TPU v7x, 128 devices: a whole 4x4x4 slice. The times are simulated.
128 devices in a mesh: dp: 16 (over x, y), seq: 8 (over z, core).
Axes of the slice: x: 4, y: 4, z: 4, core: 2. Of those that a mesh axis runs over, the one named last changes fastest.
Arguments:
- queries: bfloat16 [16, 8, 384, 1024], P('dp', 'seq'), may hold values from -6 to 6
- keys: bfloat16 [16, 8, 384, 1024], P('dp', 'seq'), may hold values from -6 to 6
- values: bfloat16 [16, 8, 384, 1024], P('dp', 'seq'), may hold values from -6 to 6
- gates: bfloat16 [16, 8, 384, 1024], P('dp', 'seq'), may hold values from -6 to 6
- attended: bfloat16 [16, 8, 384, 1024], P('dp', 'seq')
- out_grad: bfloat16 [16, 8, 384, 1024], P('dp', 'seq'), may hold values from -6 to 6
- plan: int32 [16, 8, 16], P(None, 'seq'), may hold values from 1 to 24, 256 in all within a row
- hist_len: int32 [16], P('dp'), may hold values from 512 to 2048, as said below
- block_mask: int32 [16, 16, 16], P('dp'), may hold values 0 or 1
Outputs:
- query_grad: bfloat16 [16, 8, 384, 1024], P('dp', 'seq')
- key_grad: bfloat16 [16, 8, 384, 1024], P('dp', 'seq')
- value_grad: bfloat16 [16, 8, 384, 1024], P('dp', 'seq')
- gate_grad: bfloat16 [16, 8, 384, 1024], P('dp', 'seq')
Inputs may be any that keep to these rules, and one draw needn't show every extreme that they name: For every history g and piece s, plan[g, s, :] sums to 256; some entry of each such row equals 24. `hist_len`: some history has exactly 2048 events.
All inputs are finite; a program needn't handle non-finite values. No bound on the sum of `block_mask` on one device may be relied on, other than what follows from the above.
Results may differ from a plain program's by a relative error of at most 0.0058.
Values may be sent and summed in bfloat16 or wider, within the bound.
A program may use at most 128 MiB of HBM per device.

v0:
```python
import jax
import jax.numpy as jnp
from jax import lax
from jax.sharding import PartitionSpec as P

HEADS = 8
ROWS = 256
BLOCK = 128


def layer_norm(inputs):
    center = inputs - jnp.mean(inputs, axis=-1, keepdims=True)
    spread = jnp.mean(center * center, axis=-1, keepdims=True)
    return center * lax.rsqrt(spread + 1e-05)


def flatten(array):
    return array.reshape(array.shape[2], array.shape[3])


def cut_rows(array, offset, extent, head_count):
    return array[offset : offset + extent].reshape(extent, head_count, -1)


def pair_terms(query_rows, grad_rows, key_rows, value_rows, live_weight):
    scale_qk = query_rows.shape[2] ** (-0.5)
    scores = (
        jnp.einsum("thd,shd->hts", query_rows, key_rows, preferred_element_type=jnp.float32)
        * scale_qk
    )
    sigmoid = jax.nn.sigmoid(scores)
    weight = (scores * sigmoid * live_weight[None]).astype(jnp.bfloat16)
    products = jnp.einsum("thd,shd->hts", grad_rows, value_rows, preferred_element_type=jnp.float32)
    score_grad = (
        products * (sigmoid * (1.0 + scores * (1.0 - sigmoid))) * live_weight[None]
    ).astype(jnp.bfloat16)
    query_part = (
        jnp.einsum("hts,shd->thd", score_grad, key_rows, preferred_element_type=jnp.float32)
        * scale_qk
    )
    key_part = (
        jnp.einsum("hts,thd->shd", score_grad, query_rows, preferred_element_type=jnp.float32)
        * scale_qk
    )
    value_part = jnp.einsum("hts,thd->shd", weight, grad_rows, preferred_element_type=jnp.float32)
    return (query_part, key_part, value_part)


def local(queries, keys, values, gates, attended, out_grad, plan, hist_len, block_mask):
    group_count = lax.axis_size("dp")
    capacity = queries.shape[2]
    model_width = queries.shape[3]
    slot_count = capacity // group_count
    row_count = ROWS
    head_count = HEADS
    head_size = model_width // head_count
    dp_index = lax.axis_index("dp")
    seq_index = lax.axis_index("seq")
    group_ids = jnp.arange(group_count, dtype=jnp.int32)
    slot_ids = jnp.arange(slot_count, dtype=jnp.int32)
    row_ids = jnp.arange(row_count, dtype=jnp.int32)
    my_plan = plan[:, 0, :]
    incoming = jnp.sum(jnp.where(group_ids[None, :] == dp_index, my_plan, 0), axis=1)
    valid = (slot_ids[None, :] < incoming[:, None]).reshape(capacity)
    normed, pullback = jax.vjp(layer_norm, flatten(attended).astype(jnp.float32))
    cotangent = flatten(out_grad).astype(jnp.float32) * flatten(gates).astype(jnp.float32)
    attn_grad = pullback(cotangent)[0].astype(jnp.bfloat16)
    gate_grad = jnp.where(
        valid[:, None], flatten(out_grad).astype(jnp.float32) * normed, 0.0
    ).astype(jnp.bfloat16)
    shape_slots = (group_count, slot_count, model_width)
    received = (
        lax.all_to_all(
            flatten(queries).reshape(shape_slots), "dp", split_axis=0, concat_axis=0, tiled=True
        ),
        lax.all_to_all(
            flatten(keys).reshape(shape_slots), "dp", split_axis=0, concat_axis=0, tiled=True
        ),
        lax.all_to_all(
            flatten(values).reshape(shape_slots), "dp", split_axis=0, concat_axis=0, tiled=True
        ),
        lax.all_to_all(
            attn_grad.reshape(shape_slots), "dp", split_axis=0, concat_axis=0, tiled=True
        ),
    )
    own_counts = jnp.sum(jnp.where(group_ids[:, None] == dp_index, my_plan, 0), axis=0)
    cum_incl = jnp.cumsum(own_counts)
    cum_excl = cum_incl - own_counts
    dest = jnp.sum((cum_incl[None, :] <= row_ids[:, None]).astype(jnp.int32), axis=1)
    begin = jnp.sum(jnp.where(group_ids[None, :] == dest[:, None], cum_excl[None, :], 0), axis=1)
    flat_index = dest * slot_count + row_ids - begin
    history = []
    for array in received:
        history.append(
            jnp.take(array.reshape(group_count * slot_count, model_width), flat_index, axis=0)
        )
    length = hist_len[0]
    pattern = block_mask[0].astype(jnp.float32)
    block_total = pattern.shape[0]
    inverse = 1.0 / jnp.sqrt(length.astype(jnp.float32))
    block_ids = jnp.arange(block_total, dtype=jnp.int32)

    def live_mask(query_pos, key_pos):
        query_block = query_pos // BLOCK
        key_block = key_pos // BLOCK
        onehot_query = (query_block[:, None] == block_ids[None, :]).astype(jnp.float32)
        onehot_key = (key_block[:, None] == block_ids[None, :]).astype(jnp.float32)
        blocks = jnp.dot(
            jnp.dot(onehot_query, pattern, precision=lax.Precision.HIGHEST),
            onehot_key.T,
            precision=lax.Precision.HIGHEST,
        )
        keep = (
            (key_pos[None, :] <= query_pos[:, None])
            & (query_pos[:, None] < length)
            & (key_pos[None, :] < length)
        )
        keep = keep & ((blocks > 0.5) | (query_block[:, None] == key_block[None, :]))
        return keep.astype(jnp.float32) * inverse

    own_pos = seq_index * row_count + row_ids
    own_query = history[0].reshape(row_count, head_count, head_size)
    own_key = history[1].reshape(row_count, head_count, head_size)
    own_value = history[2].reshape(row_count, head_count, head_size)
    own_grad = history[3].reshape(row_count, head_count, head_size)
    zeros = jnp.zeros((row_count, head_count, head_size), jnp.float32)
    anchor = jnp.int32(0)
    shard_query = lax.all_gather(history[0], "seq", axis=0, tiled=True)
    shard_key = lax.all_gather(history[1], "seq", axis=0, tiled=True)
    shard_value = lax.all_gather(history[2], "seq", axis=0, tiled=True)
    shard_grad = lax.all_gather(history[3], "seq", axis=0, tiled=True)
    total = shard_query.shape[0]
    query_sum = zeros
    key_sum = zeros
    value_sum = zeros
    for offset in range(0, total, 1024):
        extent = min(1024, total - offset)
        positions = anchor + offset + jnp.arange(extent, dtype=jnp.int32)
        part_query = cut_rows(shard_query, offset, extent, head_count)
        part_key = cut_rows(shard_key, offset, extent, head_count)
        part_value = cut_rows(shard_value, offset, extent, head_count)
        part_grad = cut_rows(shard_grad, offset, extent, head_count)
        earlier = pair_terms(
            own_query, own_grad, part_key, part_value, live_mask(own_pos, positions)
        )
        later = pair_terms(part_query, part_grad, own_key, own_value, live_mask(positions, own_pos))
        query_sum = query_sum + earlier[0]
        key_sum = key_sum + later[1]
        value_sum = value_sum + later[2]
    sums = (query_sum, key_sum, value_sum)
    grads = [array.astype(jnp.bfloat16).reshape(row_count, model_width) for array in sums]
    row_index = jnp.minimum(cum_excl[:, None] + slot_ids[None, :], row_count - 1).reshape(-1)
    keep_slots = (slot_ids[None, :] < own_counts[:, None]).reshape(-1)

    def pack(array):
        picked = jnp.take(array, row_index, axis=0)
        return jnp.where(keep_slots[:, None], picked, 0.0).reshape(shape_slots)

    returned = (
        lax.all_to_all(pack(grads[0]), "dp", split_axis=0, concat_axis=0, tiled=True),
        lax.all_to_all(pack(grads[1]), "dp", split_axis=0, concat_axis=0, tiled=True),
        lax.all_to_all(pack(grads[2]), "dp", split_axis=0, concat_axis=0, tiled=True),
    )
    out_shape = (1, 1, capacity, model_width)
    return (
        returned[0].reshape(out_shape),
        returned[1].reshape(out_shape),
        returned[2].reshape(out_shape),
        gate_grad.reshape(out_shape),
    )


def solution(mesh):
    in_specs = (
        P("dp", "seq", None, None),
        P("dp", "seq", None, None),
        P("dp", "seq", None, None),
        P("dp", "seq", None, None),
        P("dp", "seq", None, None),
        P("dp", "seq", None, None),
        P(None, "seq", None),
        P("dp"),
        P("dp", None, None),
    )
    out_specs = (
        P("dp", "seq", None, None),
        P("dp", "seq", None, None),
        P("dp", "seq", None, None),
        P("dp", "seq", None, None),
    )
    return jax.shard_map(local, mesh=mesh, in_specs=in_specs, out_specs=out_specs, check_vma=False)
```

profile of v0, /device:TPU:0, one launch (start us, length us, event | category | flops | bytes accessed | tf_op | source)
XLA Modules:
  0.0 369.2 jit_solution(3230899232040963151)
XLA Ops:
  17.8 21.0 %all_to_all.35 = bf16[16,24,1024]{2,1,0:T(8,128)(2,1)S(1)} all-to-all(bf16[16,24,1024]{2,1,0:T(8,128)(2,1)S(1)} %fusion.17), channel_id=1, replica_groups=mesh['dp'=16,'seq'=8] {'dp'}, dimensions={0} | all-to-all | bytes 1572864 | tf_op jit(solution)/shard_map/all_to_all | solution.py:82
  38.8 16.4 %all_to_all.36 = bf16[16,24,1024]{2,1,0:T(8,128)(2,1)S(1)} all-to-all(bf16[16,24,1024]{2,1,0:T(8,128)(2,1)S(1)} %bitcast.158), channel_id=1, replica_groups=mesh['dp'=16,'seq'=8] {'dp'}, dimensions={0} | all-to-all | bytes 1572864 | tf_op jit(solution)/shard_map/all_to_all | solution.py:76
  55.2 15.4 %all_to_all.37 = bf16[16,24,1024]{2,1,0:T(8,128)(2,1)S(1)} all-to-all(bf16[16,24,1024]{2,1,0:T(8,128)(2,1)} %bitcast.159), channel_id=1, replica_groups=mesh['dp'=16,'seq'=8] {'dp'}, dimensions={0} | all-to-all | bytes 1572864 | tf_op jit(solution)/shard_map/all_to_all | solution.py:79
  70.6 3.6 all-to-all-start.3
  79.8 5.9 %all-to-all-done.3 = bf16[16,24,1024]{2,1,0:T(8,128)(2,1)S(1)} async-done(((bf16[16,24,1024]{2,1,0:T(8,128)(2,1)}), bf16[16,24,1024]{2,1,0:T(8,128)(2,1)S(1)}, u32[]{:S(2)}, u32[]{:S(2)}) %all-to-all-start.3) | async-done | bytes 786464 | tf_op jit(solution)/shard_map/all_to_all | solution.py:73
  101.1 18.8 %all-gather.7.cloned.1.call-done = bf16[2048,1024]{1,0:T(8,128)(2,1)} async-done(((bf16[256,1024]{1,0:T(8,128)(2,1)}), bf16[2048,1024]{1,0:T(8,128)(2,1)}) %all-gather.7.cloned.1.call-update) | async-done | bytes 4194320 | tf_op jit(solution)/shard_map/all_gather | solution.py:130
  119.9 4.0 %fusion.111 = (bf16[1024,1024]{1,0:T(8,128)(2,1)}, bf16[1024,1024]{1,0:T(8,128)(2,1)S(1)}) fusion(bf16[2048,1024]{1,0:T(8,128)(2,1)} %all-gather.7.cloned.1.call-done), kind=kLoop, calls=%fused_computation.176 | loop fusion | bytes 8388608 | tf_op jit(solution)/shard_map/slice | solution.py:22
  124.0 2.8 copy.69
  126.8 27.6 %all-gather.9.cloned.1.call-done = bf16[2048,1024]{1,0:T(8,128)(2,1)} async-done(((bf16[256,1024]{1,0:T(8,128)(2,1)}), bf16[2048,1024]{1,0:T(8,128)(2,1)}) %all-gather.9.cloned.1.call-update) | async-done | bytes 4194320 | tf_op jit(solution)/shard_map/all_gather | solution.py:128
  154.4 4.0 %fusion.110 = (bf16[1024,1024]{1,0:T(8,128)(2,1)S(1)}, bf16[1024,1024]{1,0:T(8,128)(2,1)}) fusion(bf16[2048,1024]{1,0:T(8,128)(2,1)} %all-gather.9.cloned.1.call-done), kind=kLoop, calls=%fused_computation.175 | loop fusion | bytes 8388608 | tf_op jit(solution)/shard_map/slice | solution.py:22
  158.4 3.9 %copy.81 = bf16[1024,1024]{0,1:T(8,128)(2,1)} copy(bf16[1024,1024]{1,0:T(8,128)(2,1)} %get-tuple-element.15) | data formatting | bytes 4194304 | tf_op jit(solution)/shard_map/slice | solution.py:22
  162.4 26.5 %all-gather.11.cloned.1.call-done = bf16[2048,1024]{1,0:T(8,128)(2,1)} async-done(((bf16[256,1024]{1,0:T(8,128)(2,1)}), bf16[2048,1024]{1,0:T(8,128)(2,1)}) %all-gather.11.cloned.1.call-update) | async-done | bytes 4194320 | tf_op jit(solution)/shard_map/all_gather | solution.py:131
  188.9 4.7 %fusion.109 = (bf16[1024,1024]{1,0:T(8,128)(2,1)}, bf16[1024,1024]{1,0:T(8,128)(2,1)}) fusion(bf16[2048,1024]{1,0:T(8,128)(2,1)} %all-gather.11.cloned.1.call-done), kind=kLoop, calls=%fused_computation.174 | loop fusion | bytes 8388608 | tf_op jit(solution)/shard_map/slice | solution.py:22
  193.6 4.0 %copy.82 = bf16[1024,1024]{0,1:T(8,128)(2,1)} copy(bf16[1024,1024]{1,0:T(8,128)(2,1)} %get-tuple-element.13) | data formatting | bytes 4194304 | tf_op jit(solution)/shard_map/slice | solution.py:22
  197.6 6.3 %fusion.58 = f32[8,256,1024]{2,1,0:T(8,128)} fusion(bf16[1024,8,128]{0,2,1:T(8,128)(2,1)} %bitcast.140, bf16[256,1024]{1,0:T(8,128)(2,1)S(1)} %copy-done.5), kind=kOutput, calls=%fused_computation.83 | convolution fusion | flops 536870912 | bytes 11010048 | tf_op jit(solution)/shard_map/thd,shd->hts/dot_general | solution.py:33
  205.3 3.2 copy-done.1
  208.5 4.1 %fusion = f32[8,128,256]{2,1,0:T(8,128)} fusion(bf16[1024,8,128]{0,2,1:T(8,128)(2,1)S(1)} %bitcast.157, f32[8,1024,256]{2,1,0:T(8,128)S(1)} %fusion.46, f32[1024,256]{1,0:T(8,128)S(1)} %copy-done.16), kind=kOutput, calls=%fused_computation.15 | convolution fusion | flops 551550976 | bytes 12582912 | tf_op jit(solution)/shard_map/hts,thd->shd/dot_general | solution.py:45
  212.6 10.7 %fusion.4 = f32[8,128,256]{2,1,0:T(8,128)} fusion(bf16[1024,8,128]{0,2,1:T(8,128)(2,1)} %bitcast.141, f32[8,1024,256]{2,1,0:T(8,128)} %copy-done.1, f32[1024,256]{1,0:T(8,128)} %fusion.36, bf16[1024,8,128]{0,2,1:T(8,128)(2,1)} %bitcast.156, bf16[256,1024]{1,0:T(8,128)(2,1)} %get-tuple-element.32), kind=kOutput, calls=%fused_computation.19 | convolution fusion | flops 1096810496 | bytes 15204352 | tf_op jit(solution)/shard_map/hts,thd->shd/dot_general | solution.py:42
  223.3 4.8 %fusion.112 = (bf16[1024,1024]{1,0:T(8,128)(2,1)}, bf16[1024,1024]{1,0:T(8,128)(2,1)}) fusion(bf16[2048,1024]{1,0:T(8,128)(2,1)} %all-gather.5.cloned.1.call-done), kind=kLoop, calls=%fused_computation.177 | loop fusion | bytes 8388608 | tf_op jit(solution)/shard_map/slice | solution.py:22
  228.2 4.0 %copy.68 = bf16[1024,1024]{0,1:T(8,128)(2,1)} copy(bf16[1024,1024]{1,0:T(8,128)(2,1)} %get-tuple-element.19) | data formatting | bytes 4194304 | tf_op jit(solution)/shard_map/slice | solution.py:22
  232.1 4.3 %copy.75 = bf16[1024,1024]{0,1:T(8,128)(2,1)} copy(bf16[1024,1024]{1,0:T(8,128)(2,1)} %get-tuple-element.16) | data formatting | bytes 4194304 | tf_op jit(solution)/shard_map/slice | solution.py:22
  236.5 6.1 %fusion.56 = f32[8,256,1024]{2,1,0:T(8,128)} fusion(bf16[1024,8,128]{0,2,1:T(8,128)(2,1)} %bitcast.145, bf16[256,1024]{1,0:T(8,128)(2,1)S(1)} %copy-done.5), kind=kOutput, calls=%fused_computation.81 | convolution fusion | flops 536870912 | bytes 11010048 | tf_op jit(solution)/shard_map/thd,shd->hts/dot_general | solution.py:33
  242.5 4.0 %copy.74 = bf16[1024,1024]{0,1:T(8,128)(2,1)} copy(bf16[1024,1024]{1,0:T(8,128)(2,1)} %get-tuple-element.18) | data formatting | bytes 4194304 | tf_op jit(solution)/shard_map/slice | solution.py:22
  246.5 10.8 %fusion.2 = f32[8,128,256]{2,1,0:T(8,128)} fusion(bf16[1024,8,128]{0,2,1:T(8,128)(2,1)} %bitcast.154, f32[8,256,1024]{2,1,0:T(8,128)} %fusion.58, f32[256,1024]{1,0:T(8,128)} %fusion.30, bf16[256,1024]{1,0:T(8,128)(2,1)S(1)} %copy-done.11), kind=kOutput, calls=%fused_computation.17 | convolution fusion | flops 1096810496 | bytes 13107200 | tf_op jit(solution)/shard_map/hts,shd->thd/dot_general | solution.py:38
  257.3 10.8 %fusion.26 = bf16[8,128,256]{2,1,0:T(8,128)(2,1)} fusion(f32[8,128,256]{2,1,0:T(8,128)} %fusion.2, bf16[1024,8,128]{0,2,1:T(8,128)(2,1)} %bitcast.155, f32[8,256,1024]{2,1,0:T(8,128)} %fusion.56, f32[256,1024]{1,0:T(8,128)} %fusion.33, bf16[256,1024]{1,0:T(8,128)(2,1)S(1)} %copy-done.11), kind=kOutput, calls=%fused_computation.46 | convolution fusion | flops 1097596928 | bytes 13631488 | tf_op jit(solution)/shard_map/hts,shd->thd/dot_general | solution.py:38
  272.1 6.3 %fusion.44 = f32[8,1024,256]{2,1,0:T(8,128)} fusion(bf16[1024,8,128]{0,2,1:T(8,128)(2,1)} %bitcast.143, bf16[256,1024]{1,0:T(8,128)(2,1)S(1)} %copy-done.4), kind=kOutput, calls=%fused_computation.73 | convolution fusion | flops 536870912 | bytes 11010048 | tf_op jit(solution)/shard_map/thd,shd->hts/dot_general | solution.py:28
  281.0 9.7 %fusion.27 = bf16[8,128,256]{2,1,0:T(8,128)(2,1)S(1)} fusion(f32[8,128,256]{2,1,0:T(8,128)} %fusion.4, bf16[1024,8,128]{0,2,1:T(8,128)(2,1)} %bitcast.144, f32[8,1024,256]{2,1,0:T(8,128)} %fusion.44, f32[1024,256]{1,0:T(8,128)} %fusion.39, bf16[1024,8,128]{0,2,1:T(8,128)(2,1)} %bitcast.152, bf16[256,1024]{1,0:T(8,128)(2,1)S(1)} %copy-done.10), kind=kOutput, calls=%fused_computation.47 | convolution fusion | flops 1097596928 | bytes 15728640 | tf_op jit(solution)/shard_map/hts,thd->shd/dot_general | solution.py:42
  295.1 7.2 %fusion.25 = bf16[8,128,256]{2,1,0:T(8,128)(2,1)S(1)} fusion(f32[8,128,256]{2,1,0:T(8,128)} %fusion, bf16[1024,8,128]{0,2,1:T(8,128)(2,1)} %bitcast.153, f32[8,1024,256]{2,1,0:T(8,128)} %fusion.44, f32[1024,256]{1,0:T(8,128)} %fusion.39), kind=kOutput, calls=%fused_computation.45 | convolution fusion | flops 552075264 | bytes 13107200 | tf_op jit(solution)/shard_map/hts,thd->shd/dot_general | solution.py:45
  305.9 21.1 %all_to_all.38 = bf16[16,24,1024]{2,1,0:T(8,128)(2,1)S(1)} all-to-all(bf16[16,24,1024]{2,1,0:T(8,128)(2,1)S(1)} %bitcast.148), channel_id=1, replica_groups=mesh['dp'=16,'seq'=8] {'dp'}, dimensions={0} | all-to-all | bytes 1572864 | tf_op jit(solution)/shard_map/all_to_all | solution.py:160
  327.0 16.8 %all_to_all.39 = bf16[16,24,1024]{2,1,0:T(8,128)(2,1)S(1)} all-to-all(bf16[16,24,1024]{2,1,0:T(8,128)(2,1)S(1)} %bitcast.147), channel_id=1, replica_groups=mesh['dp'=16,'seq'=8] {'dp'}, dimensions={0} | all-to-all | bytes 1572864 | tf_op jit(solution)/shard_map/all_to_all | solution.py:161
  343.8 3.6 all-to-all-start.6
  347.5 12.4 %all-to-all-done.6 = bf16[16,24,1024]{2,1,0:T(8,128)(2,1)S(1)} async-done(((bf16[16,24,1024]{2,1,0:T(8,128)(2,1)}), bf16[16,24,1024]{2,1,0:T(8,128)(2,1)S(1)}, u32[]{:S(2)}, u32[]{:S(2)}) %all-to-all-start.6) | async-done | bytes 786464 | tf_op jit(solution)/shard_map/all_to_all | solution.py:162
  (103 shorter events, 49.0 us)
Async XLA Ops:
  7.2 6.6 %copy-start = (bf16[1,1,384,1024]{3,2,1,0:T(8,128)(2,1)S(1)}, bf16[1,1,384,1024]{3,2,1,0:T(8,128)(2,1)}, u32[]{:S(2)}) copy-start(bf16[1,1,384,1024]{3,2,1,0:T(8,128)(2,1)} %param.17) | copy-start | bytes 2359300
  7.2 6.6 %copy-start.7 = (bf16[1,1,384,1024]{3,2,1,0:T(8,128)(2,1)S(1)}, bf16[1,1,384,1024]{3,2,1,0:T(8,128)(2,1)}, u32[]{:S(2)}) copy-start(bf16[1,1,384,1024]{3,2,1,0:T(8,128)(2,1)} %param.16) | copy-start | bytes 2359300
  7.2 6.6 %copy-start.6 = (bf16[1,1,384,1024]{3,2,1,0:T(8,128)(2,1)S(1)}, bf16[1,1,384,1024]{3,2,1,0:T(8,128)(2,1)}, u32[]{:S(2)}) copy-start(bf16[1,1,384,1024]{3,2,1,0:T(8,128)(2,1)} %param.18) | copy-start | bytes 2359300
  7.2 6.3 %copy-start.14 = (s32[16,1,16]{2,1,0:T(1,128)S(1)}, s32[16,1,16]{2,1,0:T(1,128)}, u32[]{:S(2)}) copy-start(s32[16,1,16]{2,1,0:T(1,128)} %param.19) | copy-start | bytes 3076
  13.8 25.0 %copy-start.13 = (bf16[1,1,384,1024]{3,2,1,0:T(8,128)(2,1)S(1)}, bf16[1,1,384,1024]{3,2,1,0:T(8,128)(2,1)}, u32[]{:S(2)}) copy-start(bf16[1,1,384,1024]{3,2,1,0:T(8,128)(2,1)} %param.14) | copy-start | bytes 2359300
  70.6 15.1 %all-to-all-start.3 = ((bf16[16,24,1024]{2,1,0:T(8,128)(2,1)}), bf16[16,24,1024]{2,1,0:T(8,128)(2,1)S(1)}, u32[]{:S(2)}, u32[]{:S(2)}) async-start(bf16[16,24,1024]{2,1,0:T(8,128)(2,1)} %bitcast.160), calls=%async_computation.3 | async-start | bytes 1572864 | tf_op jit(solution)/shard_map/all_to_all | solution.py:73
  74.3 45.7 %all-gather.7.cloned.1.call-start = ((), (), s32[]{:S(2)}) async-start(), calls=%async_computation.8 | async-start | bytes 4718592 | tf_op jit(solution)/shard_map/all_gather | solution.py:130
  78.7 8.3 %copy-start.8 = (bf16[256,1024]{1,0:T(8,128)(2,1)S(1)}, bf16[256,1024]{1,0:T(8,128)(2,1)}, u32[]{:S(2)}) copy-start(bf16[256,1024]{1,0:T(8,128)(2,1)} %gather_fusion.1) | copy-start | bytes 1572868
  78.7 8.3 %copy-start.9 = (bf16[256,1024]{1,0:T(8,128)(2,1)S(1)}, bf16[256,1024]{1,0:T(8,128)(2,1)}, u32[]{:S(2)}) copy-start(bf16[256,1024]{1,0:T(8,128)(2,1)} %gather_fusion) | copy-start | bytes 1572868
  86.9 4.7 %copy-start.15 = (s32[1,16,16]{2,1,0:T(8,128)S(1)}, s32[1,16,16]{2,1,0:T(8,128)}, u32[]{:S(2)}) copy-start(s32[1,16,16]{2,1,0:T(8,128)} %param.21) | copy-start | bytes 3076
  88.6 65.8 %all-gather.9.cloned.1.call-start = ((), (), s32[]{:S(2)}) async-start(), calls=%async_computation.9 | async-start | bytes 4718592 | tf_op jit(solution)/shard_map/all_gather | solution.py:128
  89.3 99.5 %all-gather.11.cloned.1.call-start = ((), (), s32[]{:S(2)}) async-start(), calls=%async_computation.10 | async-start | bytes 4718592 | tf_op jit(solution)/shard_map/all_gather | solution.py:131
  90.0 133.3 %all-gather.5.cloned.1.call-start = ((), (), s32[]{:S(2)}) async-start(), calls=%async_computation.7 | async-start | bytes 4718592 | tf_op jit(solution)/shard_map/all_gather | solution.py:129
  193.6 4.0 %copy-start.5 = (bf16[256,1024]{1,0:T(8,128)(2,1)S(1)}, bf16[256,1024]{1,0:T(8,128)(2,1)}, u32[]{:S(2)}) copy-start(bf16[256,1024]{1,0:T(8,128)(2,1)} %get-tuple-element.31) | copy-start | bytes 1572868
  197.6 6.3 %copy-start.3 = (bf16[1024,1024]{0,1:T(8,128)(2,1)S(1)}, bf16[1024,1024]{0,1:T(8,128)(2,1)}, u32[]{:S(2)}) copy-start(bf16[1024,1024]{0,1:T(8,128)(2,1)} %copy.81) | copy-start | bytes 6291460
  197.6 6.3 %copy-start.4 = (bf16[256,1024]{1,0:T(8,128)(2,1)S(1)}, bf16[256,1024]{1,0:T(8,128)(2,1)}, u32[]{:S(2)}) copy-start(bf16[256,1024]{1,0:T(8,128)(2,1)} %get-tuple-element.33) | copy-start | bytes 1572868
  203.9 4.6 %copy-start.12 = (bf16[1024,1024]{0,1:T(8,128)(2,1)S(1)}, bf16[1024,1024]{0,1:T(8,128)(2,1)}, u32[]{:S(2)}) copy-start(bf16[1024,1024]{0,1:T(8,128)(2,1)} %copy.82) | copy-start | bytes 6291460
  203.9 4.6 %copy-start.16 = (f32[1024,256]{1,0:T(8,128)S(1)}, f32[1024,256]{1,0:T(8,128)}, u32[]{:S(2)}) copy-start(f32[1024,256]{1,0:T(8,128)} %fusion.36) | copy-start | bytes 3145732
  205.3 3.2 copy-start.1
  242.5 4.0 %copy-start.11 = (bf16[256,1024]{1,0:T(8,128)(2,1)S(1)}, bf16[256,1024]{1,0:T(8,128)(2,1)}, u32[]{:S(2)}) copy-start(bf16[256,1024]{1,0:T(8,128)(2,1)} %get-tuple-element.30) | copy-start | bytes 1572868
  272.1 6.3 %copy-start.2 = (bf16[1024,1024]{1,0:T(8,128)(2,1)S(1)}, bf16[1024,1024]{1,0:T(8,128)(2,1)}, u32[]{:S(2)}) copy-start(bf16[1024,1024]{1,0:T(8,128)(2,1)} %get-tuple-element.12) | copy-start | bytes 6291460
  278.4 2.7 copy-start.10
  343.8 16.0 %all-to-all-start.6 = ((bf16[16,24,1024]{2,1,0:T(8,128)(2,1)}), bf16[16,24,1024]{2,1,0:T(8,128)(2,1)S(1)}, u32[]{:S(2)}, u32[]{:S(2)}) async-start(bf16[16,24,1024]{2,1,0:T(8,128)(2,1)} %bitcast.33), calls=%async_computation.6 | async-start | bytes 1572864 | tf_op jit(solution)/shard_map/all_to_all | solution.py:162
Sparse Core Ops, SparseCore 0:
  88.7 31.2 all-gather.6
  122.2 32.1 all-gather.8
  156.7 32.1 all-gather.10
  190.4 32.1 all-gather.4
where the time goes:
time: 375 us; the launch traced here: 369 us
  waiting for transfers between devices  92.7 us (25%)
  blocking collectives  90.8 us (24%)
  matrix products  82.7 us (22%)
  local copies, waits for them, and re-layouts  66.8 us (18%)
  between operations  15 us (4%)
  other arithmetic  13.3 us (4%)
  starting transfers between devices  7.89 us (2%)
    slice x12, local copies, waits for them, and re-layouts, cut_rows(): return array[offset:offset + extent].reshape(extent, head_count, -1)  46 us
    all_gather x1, waiting for transfers between devices, local(): shard_query = lax.all_gather(history[0], 'seq', axis=0, tiled=True)  27.6 us
    all_gather x1, waiting for transfers between devices, local(): shard_grad = lax.all_gather(history[3], 'seq', axis=0, tiled=True)  26.5 us
    dot_general x2, matrix products, pair_terms(): jnp.einsum('hts,shd->thd', score_grad, key_rows, preferred_element_type=j...  21.6 us
    all_to_all x1, blocking collectives, local(): lax.all_to_all(pack(grads[0]), 'dp', split_axis=0, concat_axis=0, tiled=T...  21.1 us
    all_to_all x1, blocking collectives, local(): lax.all_to_all(attn_grad.reshape(shape_slots), 'dp', split_axis=0, concat...  21 us
    dot_general x2, matrix products, pair_terms(): jnp.einsum('hts,thd->shd', score_grad, query_rows, preferred_element_type...  20.4 us
    all_gather x1, waiting for transfers between devices, local(): shard_value = lax.all_gather(history[2], 'seq', axis=0, tiled=True)  18.8 us
  transfers between devices with their start and end apart: 6, of which 5 were waited for; matrix products, arithmetic and copies ran while one was open for 17% of the time, Pallas kernels for 0%

commit v1 on v0

--- a/solution.py
+++ b/solution.py
@@ -125,7 +125,21 @@
     own_grad = history[3].reshape(row_count, head_count, head_size)
     zeros = jnp.zeros((row_count, head_count, head_size), jnp.float32)
     anchor = jnp.int32(0)
-    shard_query = lax.all_gather(history[0], "seq", axis=0, tiled=True)
+    ways, here, step = (lax.axis_size("seq"), lax.axis_index("seq"), history[0].shape[0])
+    lengths = [n * ways if d == 0 else n for d, n in enumerate(history[0].shape)]
+    full = lax.dynamic_update_slice_in_dim(
+        jnp.zeros(lengths, history[0].dtype), history[0], here * step, axis=0
+    )
+    going_up = going_down = history[0]
+    for far in range(1, ways // 2 + 1):
+        going_up = lax.ppermute(going_up, "seq", [(d, (d + 1) % ways) for d in range(ways)])
+        full = lax.dynamic_update_slice_in_dim(full, going_up, (here - far) % ways * step, axis=0)
+        if 2 * far < ways:
+            going_down = lax.ppermute(going_down, "seq", [(d, (d - 1) % ways) for d in range(ways)])
+            full = lax.dynamic_update_slice_in_dim(
+                full, going_down, (here + far) % ways * step, axis=0
+            )
+    shard_query = full
     shard_key = lax.all_gather(history[1], "seq", axis=0, tiled=True)
     shard_value = lax.all_gather(history[2], "seq", axis=0, tiled=True)
     shard_grad = lax.all_gather(history[3], "seq", axis=0, tiled=True)

time: 375 us -> 336 us (0.90)
  the two profiles are of different devices: /device:TPU:0 before, /device:TPU:96 now
where the time goes in v1:
time: 336 us; the launch traced here: 330 us
  blocking collectives  86.4 us (26%)
  matrix products  82.4 us (25%)
  local copies, waits for them, and re-layouts  70.4 us (21%)
  waiting for transfers between devices  49.1 us (15%)
  between operations  15.3 us (5%)
  starting transfers between devices  13.3 us (4%)
  other arithmetic  13.1 us (4%)
    slice x10, local copies, waits for them, and re-layouts, cut_rows(): return array[offset:offset + extent].reshape(extent, head_count, -1)  38.4 us
    ppermute x4, waiting for transfers between devices, local(): lax.ppermute(going_up, 'seq', [(d, (d + 1) % ways) for d in range(ways)])  25.9 us
    all_to_all x1, blocking collectives, local(): lax.all_to_all(attn_grad.reshape(shape_slots), 'dp', split_axis=0, concat...  21 us
    dot_general x2, matrix products, pair_terms(): jnp.einsum('hts,thd->shd', score_grad, query_rows, preferred_element_type...  20.1 us
    dot_general x2, matrix products, pair_terms(): jnp.einsum('hts,shd->thd', score_grad, key_rows, preferred_element_type=j...  19.5 us
    all_to_all x1, blocking collectives, local(): lax.all_to_all(pack(grads[0]), 'dp', split_axis=0, concat_axis=0, tiled=T...  17 us
    all_to_all x1, blocking collectives, local(): lax.all_to_all(pack(grads[1]), 'dp', split_axis=0, concat_axis=0, tiled=T...  16.7 us
    all_to_all x1, blocking collectives, local(): lax.all_to_all(flatten(keys).reshape(shape_slots), 'dp', split_axis=0, co...  16.4 us
  transfers between devices with their start and end apart: 12, of which 6 were waited for; matrix products, arithmetic and copies ran while one was open for 29% of the time, Pallas kernels for 0%

profile of v1, /device:TPU:96, one launch (start us, length us, event | category | flops | bytes accessed | tf_op | source)
XLA Modules:
  0.0 330.0 jit_solution(12810270881341604355)
XLA Ops:
  17.8 21.0 %all_to_all.35 = bf16[16,24,1024]{2,1,0:T(8,128)(2,1)S(1)} all-to-all(bf16[16,24,1024]{2,1,0:T(8,128)(2,1)S(1)} %fusion.17), channel_id=1, replica_groups=mesh['dp'=16,'seq'=8] {'dp'}, dimensions={0} | all-to-all | bytes 1572864 | tf_op jit(solution)/shard_map/all_to_all | solution.py:82
  38.7 16.4 %all_to_all.36 = bf16[16,24,1024]{2,1,0:T(8,128)(2,1)S(1)} all-to-all(bf16[16,24,1024]{2,1,0:T(8,128)(2,1)S(1)} %bitcast.158), channel_id=1, replica_groups=mesh['dp'=16,'seq'=8] {'dp'}, dimensions={0} | all-to-all | bytes 1572864 | tf_op jit(solution)/shard_map/all_to_all | solution.py:76
  55.1 15.4 %all_to_all.37 = bf16[16,24,1024]{2,1,0:T(8,128)(2,1)S(1)} all-to-all(bf16[16,24,1024]{2,1,0:T(8,128)(2,1)} %bitcast.159), channel_id=1, replica_groups=mesh['dp'=16,'seq'=8] {'dp'}, dimensions={0} | all-to-all | bytes 1572864 | tf_op jit(solution)/shard_map/all_to_all | solution.py:79
  70.5 3.6 %all-to-all-start.3 = ((bf16[16,24,1024]{2,1,0:T(8,128)(2,1)}), bf16[16,24,1024]{2,1,0:T(8,128)(2,1)S(1)}, u32[]{:S(2)}, u32[]{:S(2)}) async-start(bf16[16,24,1024]{2,1,0:T(8,128)(2,1)} %bitcast.160), calls=%async_computation.3 | async-start | bytes 1572864 | tf_op jit(solution)/shard_map/all_to_all | solution.py:73
  79.8 5.9 %all-to-all-done.3 = bf16[16,24,1024]{2,1,0:T(8,128)(2,1)S(1)} async-done(((bf16[16,24,1024]{2,1,0:T(8,128)(2,1)}), bf16[16,24,1024]{2,1,0:T(8,128)(2,1)S(1)}, u32[]{:S(2)}, u32[]{:S(2)}) %all-to-all-start.3) | async-done | bytes 786464 | tf_op jit(solution)/shard_map/all_to_all | solution.py:73
  97.4 11.3 %collective-permute-done = bf16[256,1024]{1,0:T(8,128)(2,1)S(1)} collective-permute-done((bf16[256,1024]{1,0:T(8,128)(2,1)S(1)}, bf16[256,1024]{1,0:T(8,128)(2,1)S(1)}, u32[]{:S(2)}, u32[]{:S(2)}) %collective-permute-start) | collective-permute-done | bytes 524320 | tf_op jit(solution)/shard_map/ppermute | solution.py:135
  110.7 4.2 %collective-permute-done.1 = bf16[256,1024]{1,0:T(8,128)(2,1)S(1)} collective-permute-done((bf16[256,1024]{1,0:T(8,128)(2,1)S(1)}, bf16[256,1024]{1,0:T(8,128)(2,1)S(1)}, u32[]{:S(2)}, u32[]{:S(2)}) %collective-permute-start.1) | collective-permute-done | bytes 524320 | tf_op jit(solution)/shard_map/ppermute | solution.py:138
  117.2 6.8 %collective-permute-done.2 = bf16[256,1024]{1,0:T(8,128)(2,1)S(1)} collective-permute-done((bf16[256,1024]{1,0:T(8,128)(2,1)S(1)}, bf16[256,1024]{1,0:T(8,128)(2,1)S(1)}, u32[]{:S(2)}, u32[]{:S(2)}) %collective-permute-start.2) | collective-permute-done | bytes 524320 | tf_op jit(solution)/shard_map/ppermute | solution.py:135
  141.2 7.9 %collective-permute-done.6 = bf16[256,1024]{1,0:T(8,128)(2,1)S(1)} collective-permute-done((bf16[256,1024]{1,0:T(8,128)(2,1)S(1)}, bf16[256,1024]{1,0:T(8,128)(2,1)S(1)}, u32[]{:S(2)}, u32[]{:S(2)}) %collective-permute-start.6) | collective-permute-done | bytes 524320 | tf_op jit(solution)/shard_map/ppermute | solution.py:135
  150.1 2.8 fusion.110
  153.0 4.6 %fusion.44 = f32[8,1024,256]{2,1,0:T(8,128)} fusion(bf16[1024,8,128]{0,2,1:T(8,128)(2,1)S(1)} %bitcast.144, bf16[256,1024]{1,0:T(8,128)(2,1)S(1)} %copy-done.6), kind=kOutput, calls=%fused_computation.73 | convolution fusion | flops 536870912 | bytes 11010048 | tf_op jit(solution)/shard_map/thd,shd->hts/dot_general | solution.py:28
  157.6 4.5 %fusion.46 = f32[8,1024,256]{2,1,0:T(8,128)} fusion(bf16[1024,8,128]{0,2,1:T(8,128)(2,1)S(1)} %bitcast.142, bf16[256,1024]{1,0:T(8,128)(2,1)S(1)} %copy-done.6), kind=kOutput, calls=%fused_computation.75 | convolution fusion | flops 536870912 | bytes 11010048 | tf_op jit(solution)/shard_map/thd,shd->hts/dot_general | solution.py:28
  162.1 4.7 %fusion.111 = (bf16[1024,1024]{1,0:T(8,128)(2,1)}, bf16[1024,1024]{1,0:T(8,128)(2,1)}) fusion(bf16[2048,1024]{1,0:T(8,128)(2,1)} %all-gather.6.cloned.1.call-done), kind=kLoop, calls=%fused_computation.184 | loop fusion | bytes 8388608 | tf_op jit(solution)/shard_map/slice | solution.py:22
  166.8 2.9 copy.81
  169.7 5.0 %fusion.112 = (bf16[1024,1024]{1,0:T(8,128)(2,1)}, bf16[1024,1024]{1,0:T(8,128)(2,1)}) fusion(bf16[2048,1024]{1,0:T(8,128)(2,1)} %all-gather.4.cloned.1.call-done), kind=kLoop, calls=%fused_computation.185 | loop fusion | bytes 8388608 | tf_op jit(solution)/shard_map/slice | solution.py:22
  174.7 3.9 %copy.80 = bf16[1024,1024]{0,1:T(8,128)(2,1)} copy(bf16[1024,1024]{1,0:T(8,128)(2,1)} %get-tuple-element.19) | data formatting | bytes 4194304 | tf_op jit(solution)/shard_map/slice | solution.py:22
  178.6 4.1 %copy.87 = bf16[1024,1024]{0,1:T(8,128)(2,1)} copy(bf16[1024,1024]{1,0:T(8,128)(2,1)} %get-tuple-element.16) | data formatting | bytes 4194304 | tf_op jit(solution)/shard_map/slice | solution.py:22
  182.7 4.4 %copy.86 = bf16[1024,1024]{0,1:T(8,128)(2,1)} copy(bf16[1024,1024]{1,0:T(8,128)(2,1)} %get-tuple-element.18) | data formatting | bytes 4194304 | tf_op jit(solution)/shard_map/slice | solution.py:22
  187.1 4.5 %fusion.58 = f32[8,256,1024]{2,1,0:T(8,128)} fusion(bf16[1024,8,128]{0,2,1:T(8,128)(2,1)S(1)} %bitcast.140, bf16[256,1024]{1,0:T(8,128)(2,1)S(1)} %copy-done.5), kind=kOutput, calls=%fused_computation.83 | convolution fusion | flops 536870912 | bytes 11010048 | tf_op jit(solution)/shard_map/thd,shd->hts/dot_general | solution.py:33
  191.6 4.5 %fusion.56 = f32[8,256,1024]{2,1,0:T(8,128)} fusion(bf16[1024,8,128]{0,2,1:T(8,128)(2,1)S(1)} %bitcast.141, bf16[256,1024]{1,0:T(8,128)(2,1)S(1)} %copy-done.5), kind=kOutput, calls=%fused_computation.81 | convolution fusion | flops 536870912 | bytes 11010048 | tf_op jit(solution)/shard_map/thd,shd->hts/dot_general | solution.py:33
  196.1 9.5 %fusion.2 = f32[8,128,256]{2,1,0:T(8,128)} fusion(bf16[1024,8,128]{0,2,1:T(8,128)(2,1)S(1)} %bitcast.154, f32[8,256,1024]{2,1,0:T(8,128)} %fusion.58, f32[256,1024]{1,0:T(8,128)} %fusion.30, bf16[256,1024]{1,0:T(8,128)(2,1)S(1)} %get-tuple-element.30), kind=kOutput, calls=%fused_computation.17 | convolution fusion | flops 1096810496 | bytes 13107200 | tf_op jit(solution)/shard_map/hts,shd->thd/dot_general | solution.py:38
  205.6 10.0 %fusion.26 = bf16[8,128,256]{2,1,0:T(8,128)(2,1)S(1)} fusion(f32[8,128,256]{2,1,0:T(8,128)} %fusion.2, bf16[1024,8,128]{0,2,1:T(8,128)(2,1)} %bitcast.155, f32[8,256,1024]{2,1,0:T(8,128)} %fusion.56, f32[256,1024]{1,0:T(8,128)} %fusion.33, bf16[256,1024]{1,0:T(8,128)(2,1)S(1)} %get-tuple-element.30), kind=kOutput, calls=%fused_computation.46 | convolution fusion | flops 1097596928 | bytes 13631488 | tf_op jit(solution)/shard_map/hts,shd->thd/dot_general | solution.py:38
  215.9 4.1 %fusion.109 = (bf16[1024,1024]{1,0:T(8,128)(2,1)S(1)}, bf16[1024,1024]{1,0:T(8,128)(2,1)}) fusion(bf16[2048,1024]{1,0:T(8,128)(2,1)} %all-gather.8.cloned.1.call-done), kind=kLoop, calls=%fused_computation.182 | loop fusion | bytes 8388608 | tf_op jit(solution)/shard_map/slice | solution.py:22
  220.0 4.0 %copy.106 = bf16[1024,1024]{0,1:T(8,128)(2,1)} copy(bf16[1024,1024]{1,0:T(8,128)(2,1)} %get-tuple-element.13) | data formatting | bytes 4194304 | tf_op jit(solution)/shard_map/slice | solution.py:22
  226.5 10.3 %fusion.5 = f32[8,128,256]{2,1,0:T(8,128)} fusion(bf16[1024,8,128]{0,2,1:T(8,128)(2,1)} %bitcast.145, f32[8,1024,256]{2,1,0:T(8,128)} %fusion.44, f32[1024,256]{1,0:T(8,128)} %fusion.39, bf16[1024,8,128]{0,2,1:T(8,128)(2,1)} %bitcast.152, bf16[256,1024]{1,0:T(8,128)(2,1)S(1)} %copy-done.11), kind=kOutput, calls=%fused_computation.20 | convolution fusion | flops 1096810496 | bytes 15204352 | tf_op jit(solution)/shard_map/hts,thd->shd/dot_general | solution.py:42
  236.8 8.0 %fusion = f32[8,128,256]{2,1,0:T(8,128)} fusion(bf16[1024,8,128]{0,2,1:T(8,128)(2,1)} %bitcast.156, f32[8,1024,256]{2,1,0:T(8,128)} %fusion.46, f32[1024,256]{1,0:T(8,128)} %fusion.36), kind=kOutput, calls=%fused_computation.15 | convolution fusion | flops 551550976 | bytes 12582912 | tf_op jit(solution)/shard_map/hts,thd->shd/dot_general | solution.py:45
  244.9 9.8 %fusion.27 = bf16[8,128,256]{2,1,0:T(8,128)(2,1)} fusion(f32[8,128,256]{2,1,0:T(8,128)} %fusion.5, bf16[1024,8,128]{0,2,1:T(8,128)(2,1)S(1)} %bitcast.143, f32[8,1024,256]{2,1,0:T(8,128)} %fusion.46, f32[1024,256]{1,0:T(8,128)} %fusion.36, bf16[1024,8,128]{0,2,1:T(8,128)(2,1)} %bitcast.157, bf16[256,1024]{1,0:T(8,128)(2,1)S(1)} %copy-done.11), kind=kOutput, calls=%fused_computation.47 | convolution fusion | flops 1097596928 | bytes 15728640 | tf_op jit(solution)/shard_map/hts,thd->shd/dot_general | solution.py:42
  260.3 7.2 %fusion.25 = bf16[8,128,256]{2,1,0:T(8,128)(2,1)S(1)} fusion(f32[8,128,256]{2,1,0:T(8,128)} %fusion, bf16[1024,8,128]{0,2,1:T(8,128)(2,1)} %bitcast.153, f32[8,1024,256]{2,1,0:T(8,128)} %fusion.44, f32[1024,256]{1,0:T(8,128)} %fusion.39), kind=kOutput, calls=%fused_computation.45 | convolution fusion | flops 552075264 | bytes 13107200 | tf_op jit(solution)/shard_map/hts,thd->shd/dot_general | solution.py:45
  271.0 17.0 %all_to_all.38 = bf16[16,24,1024]{2,1,0:T(8,128)(2,1)S(1)} all-to-all(bf16[16,24,1024]{2,1,0:T(8,128)(2,1)S(1)} %bitcast.148), channel_id=1, replica_groups=mesh['dp'=16,'seq'=8] {'dp'}, dimensions={0} | all-to-all | bytes 1572864 | tf_op jit(solution)/shard_map/all_to_all | solution.py:174
  288.0 16.7 %all_to_all.39 = bf16[16,24,1024]{2,1,0:T(8,128)(2,1)S(1)} all-to-all(bf16[16,24,1024]{2,1,0:T(8,128)(2,1)S(1)} %bitcast.147), channel_id=1, replica_groups=mesh['dp'=16,'seq'=8] {'dp'}, dimensions={0} | all-to-all | bytes 1572864 | tf_op jit(solution)/shard_map/all_to_all | solution.py:175
  304.7 3.6 %all-to-all-start.6 = ((bf16[16,24,1024]{2,1,0:T(8,128)(2,1)}), bf16[16,24,1024]{2,1,0:T(8,128)(2,1)S(1)}, u32[]{:S(2)}, u32[]{:S(2)}) async-start(bf16[16,24,1024]{2,1,0:T(8,128)(2,1)} %bitcast.33), calls=%async_computation.6 | async-start | bytes 1572864 | tf_op jit(solution)/shard_map/all_to_all | solution.py:176
  308.4 12.2 %all-to-all-done.6 = bf16[16,24,1024]{2,1,0:T(8,128)(2,1)S(1)} async-done(((bf16[16,24,1024]{2,1,0:T(8,128)(2,1)}), bf16[16,24,1024]{2,1,0:T(8,128)(2,1)S(1)}, u32[]{:S(2)}, u32[]{:S(2)}) %all-to-all-start.6) | async-done | bytes 786464 | tf_op jit(solution)/shard_map/all_to_all | solution.py:176
  (129 shorter events, 63.9 us)
Async XLA Ops:
  7.2 6.6 %copy-start = (bf16[1,1,384,1024]{3,2,1,0:T(8,128)(2,1)S(1)}, bf16[1,1,384,1024]{3,2,1,0:T(8,128)(2,1)}, u32[]{:S(2)}) copy-start(bf16[1,1,384,1024]{3,2,1,0:T(8,128)(2,1)} %param.17) | copy-start | bytes 2359300
  7.2 6.6 %copy-start.8 = (bf16[1,1,384,1024]{3,2,1,0:T(8,128)(2,1)S(1)}, bf16[1,1,384,1024]{3,2,1,0:T(8,128)(2,1)}, u32[]{:S(2)}) copy-start(bf16[1,1,384,1024]{3,2,1,0:T(8,128)(2,1)} %param.16) | copy-start | bytes 2359300
  7.2 6.6 %copy-start.7 = (bf16[1,1,384,1024]{3,2,1,0:T(8,128)(2,1)S(1)}, bf16[1,1,384,1024]{3,2,1,0:T(8,128)(2,1)}, u32[]{:S(2)}) copy-start(bf16[1,1,384,1024]{3,2,1,0:T(8,128)(2,1)} %param.18) | copy-start | bytes 2359300
  7.2 6.3 %copy-start.15 = (s32[16,1,16]{2,1,0:T(1,128)S(1)}, s32[16,1,16]{2,1,0:T(1,128)}, u32[]{:S(2)}) copy-start(s32[16,1,16]{2,1,0:T(1,128)} %param.19) | copy-start | bytes 3076
  13.8 24.9 %copy-start.13 = (bf16[1,1,384,1024]{3,2,1,0:T(8,128)(2,1)S(1)}, bf16[1,1,384,1024]{3,2,1,0:T(8,128)(2,1)}, u32[]{:S(2)}) copy-start(bf16[1,1,384,1024]{3,2,1,0:T(8,128)(2,1)} %param.14) | copy-start | bytes 2359300
  70.5 15.1 %all-to-all-start.3 = ((bf16[16,24,1024]{2,1,0:T(8,128)(2,1)}), bf16[16,24,1024]{2,1,0:T(8,128)(2,1)S(1)}, u32[]{:S(2)}, u32[]{:S(2)}) async-start(bf16[16,24,1024]{2,1,0:T(8,128)(2,1)} %bitcast.160), calls=%async_computation.3 | async-start | bytes 1572864 | tf_op jit(solution)/shard_map/all_to_all | solution.py:73
  74.2 87.9 %all-gather.6.cloned.1.call-start = ((), (), s32[]{:S(2)}) async-start(), calls=%async_computation.8 | async-start | bytes 4718592 | tf_op jit(solution)/shard_map/all_gather | solution.py:144
  78.6 8.3 %copy-start.9 = (bf16[256,1024]{1,0:T(8,128)(2,1)S(1)}, bf16[256,1024]{1,0:T(8,128)(2,1)}, u32[]{:S(2)}) copy-start(bf16[256,1024]{1,0:T(8,128)(2,1)} %gather_fusion.1) | copy-start | bytes 1572868
  78.6 8.3 %copy-start.10 = (bf16[256,1024]{1,0:T(8,128)(2,1)S(1)}, bf16[256,1024]{1,0:T(8,128)(2,1)}, u32[]{:S(2)}) copy-start(bf16[256,1024]{1,0:T(8,128)(2,1)} %gather_fusion) | copy-start | bytes 1572868
  85.7 4.3 %copy-start.16 = (s32[1,16,16]{2,1,0:T(8,128)S(1)}, s32[1,16,16]{2,1,0:T(8,128)}, u32[]{:S(2)}) copy-start(s32[1,16,16]{2,1,0:T(8,128)} %param.21) | copy-start | bytes 3076
  88.3 81.4 %all-gather.4.cloned.1.call-start = ((), (), s32[]{:S(2)}) async-start(), calls=%async_computation.7 | async-start | bytes 4718592 | tf_op jit(solution)/shard_map/all_gather | solution.py:143
  89.0 126.8 %all-gather.8.cloned.1.call-start = ((), (), s32[]{:S(2)}) async-start(), calls=%async_computation.9 | async-start | bytes 4718592 | tf_op jit(solution)/shard_map/all_gather | solution.py:145
  92.9 15.8 %collective-permute-start = (bf16[256,1024]{1,0:T(8,128)(2,1)S(1)}, bf16[256,1024]{1,0:T(8,128)(2,1)S(1)}, u32[]{:S(2)}, u32[]{:S(2)}) collective-permute-start(bf16[256,1024]{1,0:T(8,128)(2,1)S(1)} %get-tuple-element.30), channel_id=1, source_target_pairs={{0,1},{1,2},{2,3},{3,4},{4,5},{5,6},{6,7},{7,0},{8,9},{9,10},{10,1... | collective-permute-start | bytes 1572872 | tf_op jit(solution)/shard_map/ppermute | solution.py:135
  95.5 19.5 %collective-permute-start.1 = (bf16[256,1024]{1,0:T(8,128)(2,1)S(1)}, bf16[256,1024]{1,0:T(8,128)(2,1)S(1)}, u32[]{:S(2)}, u32[]{:S(2)}) collective-permute-start(bf16[256,1024]{1,0:T(8,128)(2,1)S(1)} %get-tuple-element.30), channel_id=1, source_target_pairs={{0,7},{1,0},{2,1},{3,2},{4,3},{5,4},{6,5},{7,6},{8,15},{9,8},{10,9... | collective-permute-start | bytes 1572872 | tf_op jit(solution)/shard_map/ppermute | solution.py:138
  108.7 15.3 %collective-permute-start.2 = (bf16[256,1024]{1,0:T(8,128)(2,1)S(1)}, bf16[256,1024]{1,0:T(8,128)(2,1)S(1)}, u32[]{:S(2)}, u32[]{:S(2)}) collective-permute-start(bf16[256,1024]{1,0:T(8,128)(2,1)S(1)} %collective-permute-done), channel_id=1, source_target_pairs={{0,1},{1,2},{2,3},{3,4},{4,5},{5,6},{6,7},{7,0},{8,9},{9,10},{10,1... | collective-permute-start | bytes 1572872 | tf_op jit(solution)/shard_map/ppermute | solution.py:135
  114.9 15.7 %copy-start.14 = (bf16[256,1024]{1,0:T(8,128)(2,1)}, bf16[256,1024]{1,0:T(8,128)(2,1)S(1)}, u32[]{:S(2)}) copy-start(bf16[256,1024]{1,0:T(8,128)(2,1)S(1)} %collective-permute-done.1) | copy-start | bytes 1572868
  114.9 11.6 %collective-permute-start.3 = (bf16[256,1024]{1,0:T(8,128)(2,1)S(1)}, bf16[256,1024]{1,0:T(8,128)(2,1)}, u32[]{:S(2)}, u32[]{:S(2)}) collective-permute-start(bf16[256,1024]{1,0:T(8,128)(2,1)S(1)} %collective-permute-done.1), channel_id=1, source_target_pairs={{0,7},{1,0},{2,1},{3,2},{4,3},{5,4},{6,5},{7,6},{8,15},{9,8},{10,9... | collective-permute-start | bytes 1572872 | tf_op jit(solution)/shard_map/ppermute | solution.py:138
  124.0 9.9 %collective-permute-start.4 = (bf16[256,1024]{1,0:T(8,128)(2,1)S(1)}, bf16[256,1024]{1,0:T(8,128)(2,1)S(1)}, u32[]{:S(2)}, u32[]{:S(2)}) collective-permute-start(bf16[256,1024]{1,0:T(8,128)(2,1)S(1)} %collective-permute-done.2), channel_id=1, source_target_pairs={{0,1},{1,2},{2,3},{3,4},{4,5},{5,6},{6,7},{7,0},{8,9},{9,10},{10,1... | collective-permute-start | bytes 1572872 | tf_op jit(solution)/shard_map/ppermute | solution.py:135
  126.5 11.6 %collective-permute-start.5 = (bf16[256,1024]{1,0:T(8,128)(2,1)}, bf16[256,1024]{1,0:T(8,128)(2,1)}, u32[]{:S(2)}, u32[]{:S(2)}) collective-permute-start(bf16[256,1024]{1,0:T(8,128)(2,1)} %collective-permute-done.3), channel_id=1, source_target_pairs={{0,7},{1,0},{2,1},{3,2},{4,3},{5,4},{6,5},{7,6},{8,15},{9,8},{10,9... | collective-permute-start | bytes 1572872 | tf_op jit(solution)/shard_map/ppermute | solution.py:138
  133.9 15.2 %collective-permute-start.6 = (bf16[256,1024]{1,0:T(8,128)(2,1)S(1)}, bf16[256,1024]{1,0:T(8,128)(2,1)S(1)}, u32[]{:S(2)}, u32[]{:S(2)}) collective-permute-start(bf16[256,1024]{1,0:T(8,128)(2,1)S(1)} %collective-permute-done.4), channel_id=1, source_target_pairs={{0,1},{1,2},{2,3},{3,4},{4,5},{5,6},{6,7},{7,0},{8,9},{9,10},{10,1... | collective-permute-start | bytes 1572872 | tf_op jit(solution)/shard_map/ppermute | solution.py:135
  150.1 2.8 copy-start.6
  152.9 4.6 %copy-start.4 = (bf16[1024,1024]{0,1:T(8,128)(2,1)}, bf16[1024,1024]{0,1:T(8,128)(2,1)S(1)}, u32[]{:S(2)}) copy-start(bf16[1024,1024]{0,1:T(8,128)(2,1)S(1)} %get-tuple-element.15) | copy-start | bytes 6291460
  152.9 4.6 %copy-start.2 = (bf16[1024,1024]{0,1:T(8,128)(2,1)}, bf16[1024,1024]{0,1:T(8,128)(2,1)S(1)}, u32[]{:S(2)}) copy-start(bf16[1024,1024]{0,1:T(8,128)(2,1)S(1)} %get-tuple-element.14) | copy-start | bytes 6291460
  178.6 8.5 %copy-start.5 = (bf16[256,1024]{1,0:T(8,128)(2,1)S(1)}, bf16[256,1024]{1,0:T(8,128)(2,1)}, u32[]{:S(2)}) copy-start(bf16[256,1024]{1,0:T(8,128)(2,1)} %get-tuple-element.31) | copy-start | bytes 1572868
  187.1 4.5 %copy-start.1 = (bf16[1024,1024]{0,1:T(8,128)(2,1)S(1)}, bf16[1024,1024]{0,1:T(8,128)(2,1)}, u32[]{:S(2)}) copy-start(bf16[1024,1024]{0,1:T(8,128)(2,1)} %copy.87) | copy-start | bytes 6291460
  191.6 4.5 %copy-start.12 = (bf16[1024,1024]{0,1:T(8,128)(2,1)S(1)}, bf16[1024,1024]{0,1:T(8,128)(2,1)}, u32[]{:S(2)}) copy-start(bf16[1024,1024]{0,1:T(8,128)(2,1)} %copy.80) | copy-start | bytes 6291460
  220.0 6.5 %copy-start.11 = (bf16[256,1024]{1,0:T(8,128)(2,1)S(1)}, bf16[256,1024]{1,0:T(8,128)(2,1)}, u32[]{:S(2)}) copy-start(bf16[256,1024]{1,0:T(8,128)(2,1)} %get-tuple-element.32) | copy-start | bytes 1572868
  236.8 8.0 %copy-start.3 = (bf16[1024,1024]{0,1:T(8,128)(2,1)S(1)}, bf16[1024,1024]{0,1:T(8,128)(2,1)}, u32[]{:S(2)}) copy-start(bf16[1024,1024]{0,1:T(8,128)(2,1)} %copy-done.2) | copy-start | bytes 6291460
  304.7 15.9 %all-to-all-start.6 = ((bf16[16,24,1024]{2,1,0:T(8,128)(2,1)}), bf16[16,24,1024]{2,1,0:T(8,128)(2,1)S(1)}, u32[]{:S(2)}, u32[]{:S(2)}) async-start(bf16[16,24,1024]{2,1,0:T(8,128)(2,1)} %bitcast.33), calls=%async_computation.6 | async-start | bytes 1572864 | tf_op jit(solution)/shard_map/all_to_all | solution.py:176
Sparse Core Ops, SparseCore 0:
  88.4 34.9 all-gather.5
  125.7 35.2 all-gather.3
  163.3 28.7 all-gather.7
